TPU v7x, 256 devices: a whole 4x4x8 slice. The times are simulated.
256 devices in a mesh: row: 4 (over x), col: 16 (over z, core), rep: 4 (over y).
Axes of the slice: x: 4, y: 4, z: 8, core: 2. Of those that a mesh axis runs over, the one named last changes fastest.
Arguments:
- right_side: float32 [4, 5, 16, 64, 128], P('rep', None, 'row'), may hold values from -6 to 6
- top_right_side: float32 [2, 16, 64, 128], P(None, 'row'), may hold values from -6 to 6
- leaf_upper: bfloat16 [4, 10, 16, 16, 128, 128], P('rep', None, 'col', 'row'), may hold values from -0.125 to 0.125
- leaf_upper_mask: int32 [4, 10, 16, 16], P('rep', None, 'col', 'row'), may hold values from 0 to 1, as said below
- leaf_lower: bfloat16 [4, 10, 16, 16, 128, 128], P('rep', None, 'col', 'row'), may hold values from -0.125 to 0.125
- leaf_lower_mask: int32 [4, 10, 16, 16], P('rep', None, 'col', 'row'), may hold values from 0 to 1, as said below
- cross_upper: bfloat16 [4, 5, 16, 2, 16, 128, 128], P('rep', None, 'col', None, 'row'), may hold values from -0.0625 to 0.0625
- cross_upper_mask: int32 [4, 5, 16, 2, 16], P('rep', None, 'col', None, 'row'), may hold values from 0 to 1, as said below
- cross_lower: bfloat16 [4, 2, 16, 5, 16, 128, 128], P('rep', None, 'col', None, 'row'), may hold values from -0.21875 to 0.21875
- cross_lower_mask: int32 [4, 2, 16, 5, 16], P('rep', None, 'col', None, 'row'), may hold values from 0 to 1, as said below
- top_upper: bfloat16 [1, 16, 16, 128, 128], P(None, 'col', 'row'), may hold values from -0.125 to 0.125
- top_lower: bfloat16 [1, 16, 16, 128, 128], P(None, 'col', 'row'), may hold values from -0.125 to 0.125
- leaf_upper_inverse: float32 [4, 5, 16, 128, 128], P('rep', None, 'row'), as said below
- leaf_lower_inverse: float32 [4, 5, 16, 128, 128], P('rep', None, 'row'), as said below
- top_upper_inverse: float32 [2, 16, 128, 128], P(None, 'row'), as said below
- top_lower_inverse: float32 [2, 16, 128, 128], P(None, 'row'), as said below
- leaf_sizes: int32 [4, 5, 16], P('rep', None, 'row'), may hold values from 32 to 128, as said below
- top_sizes: int32 [2, 16], P(None, 'row'), may hold values from 32 to 128, as said below
Outputs:
- solution: float32 [4, 5, 16, 64, 128], P('rep', None, 'row', 'col')
- top_solution: float32 [2, 16, 64, 128], P(None, 'row', 'col')
Inputs may be any that keep to these rules, and one draw needn't show every extreme that they name: `leaf_sizes`: cell counts of the supernodes; the largest and the smallest are each reached in every draw. `top_sizes`: cell counts of the supernodes; the largest and the smallest are each reached in every draw. `leaf_upper_mask`: every supernode has one parent in the next level of the elimination tree (the top leaf level's parents lie in the lowest ancestor level, and ancestors' parents are common to all subtrees); the block pattern is 1 where the later level's supernode is an ancestor of the earlier level's supernode, plus some further fill blocks, else 0; L and U patterns follow the same tree. `leaf_lower_mask`: 1 where the consumed (later level's) supernode is an ancestor of the produced one in the elimination tree, plus some further fill blocks, else 0. `cross_upper_mask`: 1 where the ancestor-level supernode is an ancestor of the leaf supernode in the elimination tree, plus some further fill blocks, else 0. `cross_lower_mask`: 1 where the ancestor-level supernode is an ancestor of the leaf supernode in the elimination tree, plus some further fill blocks, else 0. `leaf_upper_inverse`: each block is the inverse of an upper triangular diagonal block, so it is upper triangular. `leaf_lower_inverse`: each block is the inverse of a unit lower triangular diagonal block, so it is unit lower triangular. `top_upper_inverse`: each block is the inverse of an upper triangular diagonal block, so it is upper triangular. `top_lower_inverse`: each block is the inverse of a unit lower triangular diagonal block, so it is unit lower triangular.
All inputs are finite; a program needn't handle non-finite values.
Results may differ from a plain program's by a relative error of at most 0.014.
Values may be sent and summed in bfloat16 or wider, within the bound.
A program may use at most 64 MiB of HBM per device.

v0:
```python
import jax
import jax.numpy as jnp
from jax import lax
from jax.experimental import pallas as pl
from jax.experimental.pallas import tpu as pltpu
from jax.sharding import PartitionSpec as P

MESH = pl.DeviceIdType.MESH
BF = jnp.bfloat16
F32 = jnp.float32

LU, CU, CL, LL, TU, TL = 0, 10, 20, 30, 40, 41
LUI, LLI, TUI, TLI = 0, 5, 10, 12


def upper_pair(m, l):
    return LU + l * (l - 1) // 2 + m


def lower_pair(l, m):
    q = 4 - l
    return LL + q * (q - 1) // 2 + (m - l - 1)


TURNED = (
    (upper_pair(1, 2), LUI + 2),
    (upper_pair(3, 4), LUI + 4),
    (TL, TLI),
    (lower_pair(3, 4), LLI + 3),
    (lower_pair(1, 2), LLI + 1),
)


def kernel(
    rs, trs, lu, ll, cu, cl, tu, tl, lui, lli, tui, tli,
    lum, llm, cum, clm, ls, ts,
    out,
    blk, inv_raw, inv, rhs, trhs, acc, y_keep, base,
    turn_out, relay, turn,
    s_z, r_z, s_x, r_x, s_zr, r_zr, r_d,
    s_cross, r_cross, s_top0, r_top0, s_mid, r_mid, r_low, xt1,
    s_last, r_last, s_out, r_out,
    load_sem, pair_ssem, pair_rsem, z_ssem, z_rsem, x_ssem, x_rsem, zr_ssem, zr_rsem, d_ssem, d_rsem,
    v_ssem, v_rsem, t_ssem, t_rsem, ts_ssem, ts_rsem, top_ssem, top_rsem, out_ssem, out_rsem,
):
    x = lax.axis_index("row")
    c = lax.axis_index("col")
    r = lax.axis_index("rep")
    z, h = c // 2, lax.rem(c, 2)
    even = lax.rem(z, 2) == 0
    first_k = 2 * lax.rem(z, 2)
    sibling = {"col": c + 1 - 2 * h}
    is_owner = (z // 2) == x
    owner = jnp.where(is_owner, 1.0, 0.0).astype(F32)
    low = jnp.where(z == 2 * x, 1.0, 0.0).astype(F32)
    high = jnp.where(z == 2 * x + 1, 1.0, 0.0).astype(F32)

    def row(d):
        return lax.rem(x + d, 4)

    def chip(d):
        return 2 * lax.rem(z + d, 8) + h

    half = pl.ds(pl.multiple_of(32 * h, 32), 32)
    loads = {}

    def load(name, src, dst):
        copy = pltpu.make_async_copy(src, dst, load_sem.at[len(loads)])
        copy.start()
        loads[name] = copy

    load("lui0", lui.at[0, pl.ds(0, 1)], inv_raw.at[pl.ds(LUI, 1)])
    load("rhs", rs.at[0, :, :, half], rhs)
    load("lu", lu.at[0, pl.ds(0, 3), 0], blk.at[pl.ds(LU, 3), h])
    load("lui", lui.at[0, pl.ds(1, 2)], inv_raw.at[pl.ds(LUI + 1, 2)])
    load("lu later", lu.at[0, pl.ds(3, 7), 0], blk.at[pl.ds(LU + 3, 7), h])
    load("lui later", lui.at[0, pl.ds(3, 2)], inv_raw.at[pl.ds(LUI + 3, 2)])
    for m in range(5):
        load(("cu", m), cu.at[0, m, 0], blk.at[pl.ds(CU + 2 * m, 2), h])
    load("trhs", trs.at[:, :, half], trhs)
    load("tui", tui, inv_raw.at[pl.ds(TUI, 2)])
    load("tli", tli, inv_raw.at[pl.ds(TLI, 2)])
    load("tu", tu.at[0], blk.at[pl.ds(TU, 1), h])
    load("tl", tl.at[0], blk.at[pl.ds(TL, 1), h])
    for a in range(2):
        load(("cl", a), cl.at[0, a, 0], blk.at[pl.ds(CL + 5 * a, 5), h])
    load("lli", lli.at[0], inv_raw.at[pl.ds(LLI, 5)])
    load("ll", ll.at[0, :, 0], blk.at[pl.ds(LL, 10), h])

    barrier = pltpu.get_barrier_semaphore()

    def greet(device):
        pl.semaphore_signal(barrier, inc=1, device_id=device, device_id_type=MESH)

    for d in (4, 3, 5, 2, 6, 1, 7):
        greet({"col": chip(d)})
    for d in (2, 1, 3):
        greet({"row": row(d)})
        greet({"rep": lax.rem(r + d, 4)})
    greet(sibling)

    def barrier_wait():
        pl.semaphore_wait(barrier, 14)

    def split(value):
        hi = value.astype(BF)
        return hi, (value - hi.astype(F32)).astype(BF)

    def masked_inverse(place, k, size):
        value = inv_raw[place, k]
        down = lax.broadcasted_iota(jnp.int32, (128, 128), 0)
        across = lax.broadcasted_iota(jnp.int32, (128, 128), 1)
        return jnp.where(jnp.maximum(down, across) < size, value, 0.0)

    def keep_inverse(place, k, value):
        hi, lo = split(value)
        inv[place, k, :, 0:128] = hi
        inv[place, k, :, 128:256] = lo

    def prepare_inverses(first, count, size_of):
        for i in range(count):
            for k in range(4):
                keep_inverse(first + i, k, masked_inverse(first + i, k, size_of(i, k)))

    def times_inverse(value, place, k):
        rows = value.shape[0]
        hi, lo = split(value)
        both = jnp.concatenate([hi, lo], axis=0)
        wide = jnp.dot(both, inv[place, k], preferred_element_type=F32)
        return wide[:rows, :128] + wide[rows:, :128] + wide[:rows, 128:]

    def cut(value):
        return [value[:, 128 * k : 128 * (k + 1)] for k in range(value.shape[1] // 128)]

    def apply_inverses(value, place):
        return [times_inverse(part, place, k) for k, part in enumerate(cut(value))]

    def own_pair_inverse(pair, place):
        return jnp.concatenate(
            [times_inverse(part, place, first_k + i) for i, part in enumerate(cut(pair))], axis=1
        )

    def contract(vectors, pair):
        columns = [
            jnp.concatenate([blk[pair, 0, k], blk[pair, 1, k]], axis=0) for k in range(4)
        ]
        return jnp.dot(vectors, jnp.concatenate(columns, axis=1), preferred_element_type=F32)

    def contract_turned(vectors, u):
        columns = [
            jnp.concatenate([turn[u, j, i] for j in range(4)], axis=0) for i in range(2)
        ]
        return jnp.dot(vectors, jnp.concatenate(columns, axis=1), preferred_element_type=F32)

    def mask_blocks(first, count, flag_of):
        def body(i, _):
            for k in range(4):
                flag = jnp.full((128, 128), flag_of(i, k).astype(F32), F32).astype(BF)
                blk[first + i, h, k] = blk[first + i, h, k] * flag
            return 0

        lax.fori_loop(0, count, body, 0)

    def remote_copy(src, dst, ssem, rsem, device):
        return pltpu.make_async_remote_copy(
            src_ref=src, dst_ref=dst, send_sem=ssem, recv_sem=rsem, device_id=device, device_id_type=MESH
        )

    def copy_out(src, dst, ssem, rsem, device, is_self=None):
        remote = remote_copy(src, dst, ssem, rsem, device)
        if is_self is None:
            remote.start()
            return

        @pl.when(is_self)
        def _():
            pltpu.make_async_copy(src, dst, rsem).start()

        @pl.when(jnp.logical_not(is_self))
        def _():
            remote.start()

    def await_bytes(ref, sem):
        pltpu.make_async_copy(ref, ref, sem).wait()

    shared = {}

    def share(name, first, count):
        at = len(shared)
        part = blk.at[pl.ds(first, count), h]
        copy = remote_copy(part, part, pair_ssem.at[at], pair_rsem.at[at], sibling)
        copy.start()
        shared[name] = copy

    def rows_of(source, level, scale):
        return jnp.concatenate([source[level, k] * scale for k in range(4)], axis=1)

    def owned(pair):
        return jnp.concatenate([pair * low, pair * high], axis=1)

    def own_pair(value):
        return jnp.where(even, value[:, :256], value[:, 256:])

    def turn_fold(u):
        pair, place = TURNED[u]
        for k in range(4):
            wide = jnp.dot(blk[pair, h, k], inv[place, k], preferred_element_type=F32)
            turn_out[u, k] = (wide[:, :128] + wide[:, 128:]).astype(BF)

    def turn_send(u):
        for d in (2, 1, 3):
            copy_out(turn_out.at[u, d], relay.at[u, x], v_ssem.at[u], v_rsem.at[u], {"row": row(d)})
        relay[u, x] = turn_out[u, 0]

    def turn_relay(u):
        await_bytes(relay.at[u, pl.ds(0, 3)], v_ssem.at[u])
        await_bytes(relay.at[u, pl.ds(0, 3)], v_rsem.at[u])
        for d in range(4):
            source = row(d)
            k = (4 - d) % 4
            copy_out(
                relay.at[u, source], turn.at[u, lax.rem(c, 4), k % 2], t_ssem.at[u], t_rsem.at[u],
                {"row": c // 4, "col": 4 * source + 2 * (k // 2) + h},
                (z == 2 * x) if d == 0 else None,
            )

    def turn_share(u):
        await_bytes(turn.at[u, pl.ds(0, 2)], t_rsem.at[u])
        await_bytes(relay.at[u, pl.ds(0, 3)], t_ssem.at[u])

        @pl.when(z != 2 * x)
        def _():
            await_bytes(relay.at[u, 3], t_ssem.at[u])

        for j in range(2):
            part = turn.at[u, 2 * j + h]
            remote_copy(part, part, ts_ssem.at[u], ts_rsem.at[u], sibling).start()

    def turn_ready(u):
        await_bytes(turn.at[u, pl.ds(0, 2)], ts_ssem.at[u])
        await_bytes(turn.at[u, pl.ds(0, 2)], ts_rsem.at[u])

    def z_send(step, parts):
        for k in range(4):
            s_z[step, k] = parts[k].astype(BF)
        for d in (4, 3, 5, 2, 6, 1, 7):
            copy_out(s_z.at[step], r_z.at[step, z], z_ssem.at[step], z_rsem.at[step], {"col": chip(d)})

    def z_receive(step, parts):
        await_bytes(r_z.at[step, pl.ds(0, 7)], z_ssem.at[step])
        await_bytes(r_z.at[step, pl.ds(0, 7)], z_rsem.at[step])
        totals = []
        for k in range(4):
            total = parts[k]
            for d in range(1, 8):
                total = total + r_z[step, lax.rem(z + d, 8), k].astype(F32)
            totals.append(total)
        return jnp.concatenate(totals, axis=1)

    def x_send(step, pair):
        for i, part in enumerate(cut(pair)):
            s_x[step, i] = part.astype(BF)
        for d in (2, 1, 3):
            copy_out(s_x.at[step], r_x.at[step, x], x_ssem.at[step], x_rsem.at[step], {"row": row(d)})

    def x_receive(step, pair):
        await_bytes(r_x.at[step, pl.ds(0, 3)], x_ssem.at[step])
        await_bytes(r_x.at[step, pl.ds(0, 3)], x_rsem.at[step])
        totals = []
        for i, total in enumerate(cut(pair)):
            for d in range(1, 4):
                total = total + r_x[step, row(d), i].astype(F32)
            totals.append(total)
        return jnp.concatenate(totals, axis=1)

    def gather_send(u, parts):
        for k in range(4):
            s_zr[u, k // 2, k % 2] = parts[k].astype(BF)
        for q in range(2):
            @pl.when(z != 2 * x + q)
            def _(q=q):
                copy_out(
                    s_zr.at[u, q], r_zr.at[u, z], zr_ssem.at[u], zr_rsem.at[u], {"col": 4 * x + 2 * q + h}
                )
        base[...] = own_pair(jnp.concatenate(parts, axis=1))

    def gather_receive(u):
        await_bytes(s_zr.at[u, 0], zr_ssem.at[u])

        @pl.when(jnp.logical_not(is_owner))
        def _():
            await_bytes(s_zr.at[u, 1], zr_ssem.at[u])
            base[...] = jnp.zeros_like(base)

        @pl.when(is_owner)
        def _():
            await_bytes(r_zr.at[u, pl.ds(0, 7)], zr_rsem.at[u])
            for i in range(2):
                total = base[:, 128 * i : 128 * (i + 1)]
                for d in range(1, 8):
                    total = total + r_zr[u, lax.rem(z + d, 8), i].astype(F32)
                base[:, 128 * i : 128 * (i + 1)] = total

    def spread_send(u, pair):
        @pl.when(is_owner)
        def _():
            for i, part in enumerate(cut(pair)):
                r_d[u, i] = part.astype(BF)
            for d in (2, 1, 3):
                copy_out(r_d.at[u], r_d.at[u], d_ssem.at[u], d_rsem.at[u], {"row": row(d)})

    def spread_receive(u):
        @pl.when(is_owner)
        def _():
            for d in range(3):
                await_bytes(r_d.at[u], d_ssem.at[u])

        @pl.when(jnp.logical_not(is_owner))
        def _():
            await_bytes(r_d.at[u], d_rsem.at[u])

        return jnp.concatenate([r_d[u, 0], r_d[u, 1]], axis=1)

    def pack(parts, rows):
        return [jnp.concatenate([parts[2 * q][rows], parts[2 * q + 1][rows]], axis=0) for q in range(2)]

    def unpack(value):
        return jnp.concatenate([value[:8], value[8:]], axis=1)

    def from_reps(quarters):
        return jnp.concatenate(
            [jnp.concatenate([quarter[8 * k : 8 * k + 8] for quarter in quarters], axis=0) for k in range(2)],
            axis=1,
        )

    def out_send(place, value):
        for i in range(4):
            for k in range(2):
                s_out[place, i, k] = value[8 * i : 8 * (i + 1), 128 * k : 128 * (k + 1)]

        @pl.when(is_owner)
        def _():
            for d in range(8):
                n = lax.rem(lax.rem(c, 8) + d, 8)
                copy_out(
                    s_out.at[place, n // 2], r_out.at[place, lax.rem(z, 2)],
                    out_ssem.at[place], out_rsem.at[0],
                    {"col": 8 * h + n}, (c // 8 == h) if d == 0 else None,
                )

    def out_sent(place):
        @pl.when(is_owner)
        def _():
            await_bytes(s_out.at[place], out_ssem.at[place])
            await_bytes(s_out.at[place, pl.ds(0, 3)], out_ssem.at[place])

            @pl.when(c // 8 != h)
            def _():
                await_bytes(s_out.at[place, 3], out_ssem.at[place])

    def subtract(level, vectors, pair):
        acc[level] = acc[level] - contract(vectors, pair)

    loads["lui0"].wait()
    prepare_inverses(LUI, 1, lambda i, k: ls[k, i])
    loads["rhs"].wait()
    y0 = own_pair_inverse(jnp.concatenate([rhs[0, first_k], rhs[0, first_k + 1]], axis=1), LUI)
    y_keep[0] = y0
    for l in range(1, 5):
        acc[l] = rows_of(rhs, l, 0.125)
    loads["lu"].wait()
    mask_blocks(LU, 3, lambda i, k: lum[k, i])
    loads["lui"].wait()
    prepare_inverses(LUI + 1, 2, lambda i, k: ls[k, i + 1])
    turn_fold(0)
    barrier_wait()

    spread_send(0, y0)
    turn_send(0)
    for l in (1, 2):
        share(("lu", l), upper_pair(0, l), l)
    loads["lu later"].wait()
    mask_blocks(LU + 3, 7, lambda i, k: lum[k, i + 3])
    for l in (3, 4):
        share(("lu", l), upper_pair(0, l), l)
    loads["lui later"].wait()
    prepare_inverses(LUI + 3, 2, lambda i, k: ls[k, i + 3])
    for m in range(5):
        loads["cu", m].wait()
        mask_blocks(CU + 2 * m, 2, lambda i, k, m=m: cum[i, k, m])
    share("cu", CU, 10)
    loads["trhs"].wait()
    for a in range(2):
        acc[5 + a] = rows_of(trhs, a, 0.03125)
    shared["lu", 1].wait_recv()
    y0b = spread_receive(0)

    parts = apply_inverses(acc[1] - contract(y0b, upper_pair(0, 1)), LUI + 1)
    turn_relay(0)
    shared["lu", 2].wait_recv()
    gather_send(0, apply_inverses(acc[2] - contract(y0b, upper_pair(0, 2)), LUI + 2))
    z_send(0, parts)
    shared["lu", 3].wait_recv()
    shared["lu", 4].wait_recv()
    for l in (3, 4):
        subtract(l, y0b, upper_pair(0, l))
    shared["cu"].wait_recv()
    for a in range(2):
        subtract(5 + a, y0b, CU + a)
    turn_fold(1)
    turn_send(1)
    turn_share(0)
    gather_receive(0)
    turn_ready(0)
    y1 = z_receive(0, parts)

    pair = base[...] - contract_turned(y1.astype(BF), 0)
    x_send(0, pair)
    own = own_pair(y1)
    y_keep[1] = own
    spread_send(1, own)
    turn_relay(1)
    y1b = spread_receive(1)
    subtract(3, y1b, upper_pair(1, 3))
    subtract(4, y1b, upper_pair(1, 4))
    y2 = x_receive(0, pair)
    y_keep[2] = y2
    y2b = y2.astype(BF)

    parts = apply_inverses(acc[3] - contract(y2b, upper_pair(2, 3)), LUI + 3)
    gather_send(
        1,
        apply_inverses(
            acc[4] - contract(y2b, upper_pair(2, 4)), LUI + 4
        ),
    )
    z_send(1, parts)
    for a in range(2):
        acc[5 + a] = acc[5 + a] - contract(y1b, CU + 2 + a) - contract(y2b, CU + 4 + a)
    loads["tui"].wait()
    loads["tli"].wait()
    prepare_inverses(TUI, 1, lambda i, k: ts[i, k])
    prepare_inverses(TLI, 2, lambda i, k: ts[i, k])
    for k in range(4):
        upper = masked_inverse(TUI + 1, k, ts[1, k])
        keep_inverse(TUI + 1, k, times_inverse(upper, TLI + 1, k))
    turn_share(1)
    loads["lli"].wait()
    prepare_inverses(LLI, 5, lambda i, k: ls[k, i])
    loads["ll"].wait()
    mask_blocks(LL, 10, lambda i, k: llm[k, i])
    loads["tu"].wait()
    loads["tl"].wait()
    for u in (2, 3, 4):
        turn_fold(u)
        turn_send(u)
    gather_receive(1)
    turn_ready(1)
    y3 = z_receive(1, parts)

    pair = base[...] - contract_turned(y3.astype(BF), 1)
    x_send(1, pair)
    own = own_pair(y3)
    y_keep[3] = own
    spread_send(2, own)
    turn_relay(2)
    share("top", TU, 1)
    y3b = spread_receive(2)
    for a in range(2):
        subtract(5 + a, y3b, CU + 6 + a)
    y4 = x_receive(1, pair)
    y_keep[4] = y4
    y4b = y4.astype(BF)

    for a in range(2):
        parts = apply_inverses(acc[5 + a] - contract(y4b, CU + 8 + a), TUI + a)
        for rr in range(4):
            for q, packed in enumerate(pack(parts, slice(8 * rr, 8 * rr + 8))):
                s_cross[a, rr, q] = packed
        for e in (2, 1, 3):
            rr = lax.rem(r + e, 4)
            copy_out(
                s_cross.at[a, rr], r_cross.at[a, r], top_ssem.at[a], top_rsem.at[a], {"rep": rr}
            )
    for a in range(2):
        loads["cl", a].wait()
        mask_blocks(CL + 5 * a, 5, lambda i, k, a=a: clm[a, k, i])
    share("cl", CL, 10)

    def cross_receive(a):
        await_bytes(r_cross.at[a, pl.ds(0, 3)], top_ssem.at[a])
        await_bytes(r_cross.at[a, pl.ds(0, 3)], top_rsem.at[a])
        totals = []
        for q in range(2):
            total = s_cross[a, r, q]
            for e in range(1, 4):
                total = total + r_cross[a, lax.rem(r + e, 4), q]
            totals.append(total)
        return totals

    for q, packed in enumerate(cross_receive(0)):
        s_top0[q] = packed.astype(BF)
    for d in (2, 1, 3, 0):
        for q in range(2):
            copy_out(
                s_top0.at[q], r_top0.at[z], top_ssem.at[2], top_rsem.at[2],
                {"row": row(d), "col": 4 * x + 2 * q + h},
                (z == 2 * x + q) if d == 0 else None,
            )
    crossing = cross_receive(1)
    share("ll", LL, 10)
    turn_share(2)
    turn_ready(2)
    shared["top"].wait_recv()
    await_bytes(r_top0.at[pl.ds(0, 7)], top_ssem.at[2])

    @pl.when(jnp.logical_not(is_owner))
    def _():
        await_bytes(r_top0.at[7], top_ssem.at[2])

    await_bytes(r_top0, top_rsem.at[2])
    top0 = r_top0[0].astype(F32)
    for zz in range(1, 8):
        top0 = top0 + r_top0[zz].astype(F32)
    top0 = unpack(top0)

    parts = [-part for part in apply_inverses(contract(top0.astype(BF), TU), TUI + 1)]
    mine = [crossing[q] + packed for q, packed in enumerate(pack(parts, slice(0, 8)))]
    for q in range(2):
        s_mid[q] = mine[q].astype(BF)
    for d in (4, 3, 5, 2, 6, 1, 7):
        copy_out(s_mid, r_mid.at[z], top_ssem.at[3], top_rsem.at[3], {"col": chip(d)})
    top0_base = own_pair_inverse(top0, TLI) * owner
    await_bytes(r_mid.at[pl.ds(0, 7)], top_ssem.at[3])
    await_bytes(r_mid.at[pl.ds(0, 7)], top_rsem.at[3])
    for q in range(2):
        for d in range(1, 8):
            mine[q] = mine[q] + r_mid[lax.rem(z + d, 8), q].astype(F32)

    vectors = jnp.concatenate([unpack(mine[q]) for q in range(2)], axis=1).astype(BF)
    pair = top0_base - contract_turned(vectors, 2)
    here = 4 * r + x
    r_low[here] = jnp.concatenate(cut(pair), axis=0)
    for e in (2, 1, 3, 0):
        for d in (2, 1, 3, 0):
            if d or e:
                copy_out(
                    r_low.at[here], r_low.at[here], top_ssem.at[4], top_rsem.at[4],
                    {"row": row(d), "rep": lax.rem(r + e, 4)},
                )

    @pl.when(is_owner)
    def _():
        xt1[r] = jnp.where(even, mine[0], mine[1])
        for e in (2, 1, 3, 0):
            for d in (2, 1, 3, 0):
                if d or e:
                    copy_out(
                        xt1.at[r], xt1.at[r], top_ssem.at[6], top_rsem.at[6],
                        {"row": row(d), "rep": lax.rem(r + e, 4)},
                    )

    turn_relay(3)
    for l in range(5):
        acc[l] = owned(y_keep[l])
    @pl.when(is_owner)
    def _():
        for _ in range(5):
            await_bytes(xt1.at[pl.ds(0, 3)], top_ssem.at[6])
        await_bytes(xt1.at[pl.ds(0, 3)], top_rsem.at[6])

    @pl.when(jnp.logical_not(is_owner))
    def _():
        await_bytes(xt1, top_rsem.at[6])

    x_top1 = from_reps([xt1[rr] for rr in range(4)])
    xt1b = x_top1.astype(BF)
    shared["cl"].wait_recv()
    subtract(4, xt1b, CL + 9)
    subtract(3, xt1b, CL + 8)
    await_bytes(r_low.at[pl.ds(0, 15)], top_ssem.at[4])
    await_bytes(r_low.at[pl.ds(0, 15)], top_rsem.at[4])
    x_top0 = from_reps([sum(r_low[4 * rr + xx] for xx in range(4)) for rr in range(4)])
    xt0b = x_top0.astype(BF)

    parts = apply_inverses(acc[4] - contract(xt0b, CL + 4), LLI + 4)
    gather_send(
        2, apply_inverses(acc[3] - contract(xt0b, CL + 3), LLI + 3)
    )
    z_send(2, parts)
    out_send(5, x_top1)
    out_send(4, x_top0)
    for l in (2, 1, 0):
        acc[l] = acc[l] - contract(xt1b, CL + 5 + l) - contract(xt0b, CL + l)
    turn_share(3)
    gather_receive(2)
    turn_ready(3)
    x4 = z_receive(2, parts)

    pair = base[...] - contract_turned(x4.astype(BF), 3)
    x_send(2, pair)
    own = own_pair(x4)
    spread_send(3, own)
    turn_relay(4)
    out_send(3, own)
    shared["ll"].wait_recv()
    x4b = spread_receive(3)
    subtract(2, x4b, lower_pair(2, 4))
    subtract(1, x4b, lower_pair(1, 4))
    x3 = x_receive(2, pair)
    x3b = x3.astype(BF)

    parts = apply_inverses(acc[2] - contract(x3b, lower_pair(2, 3)), LLI + 2)
    gather_send(
        3,
        apply_inverses(
            acc[1] - contract(x3b, lower_pair(1, 3)), LLI + 1
        ),
    )
    z_send(3, parts)
    out_send(2, x3)
    acc[0] = acc[0] - contract(x4b, lower_pair(0, 4)) - contract(x3b, lower_pair(0, 3))
    turn_share(4)
    gather_receive(3)
    turn_ready(4)
    x2 = z_receive(3, parts)

    pair = base[...] - contract_turned(x2.astype(BF), 4)
    x_send(3, pair)
    own = own_pair(x2)
    spread_send(4, own)
    out_send(1, own)
    x2b = spread_receive(4)
    subtract(0, x2b, lower_pair(0, 2))
    x1 = x_receive(3, pair)
    x1b = x1.astype(BF)

    parts = apply_inverses(acc[0] - contract(x1b, lower_pair(0, 1)), LLI)
    for i in range(4):
        for q, packed in enumerate(pack(parts, slice(8 * i, 8 * i + 8))):
            s_last[i, q] = packed.astype(BF)
    for d in (4, 3, 5, 2, 6, 1, 7, 0):
        n = lax.rem(lax.rem(c, 8) + d, 8)
        copy_out(
            s_last.at[n // 2], r_last.at[z], top_ssem.at[7], top_rsem.at[7],
            {"col": 8 * h + n}, (c // 8 == h) if d == 0 else None,
        )
    out_send(0, x1)

    def own_rows(value):
        return jnp.where(h == 0, value[0:4], value[4:8])

    for copy in shared.values():
        copy.wait_send()
    for place in range(6):
        out_sent(place)
    await_bytes(r_last.at[pl.ds(0, 7)], top_ssem.at[7])

    @pl.when(h != c // 8)
    def _():
        await_bytes(r_last.at[7], top_ssem.at[7])

    await_bytes(r_out, out_rsem.at[0])
    for place in range(6):
        for k in range(4):
            value = own_rows(r_out[place, k // 2, k % 2])
            if place == 5:
                out[6, k] = value
            elif place == 4:
                out[5, k] = value
            else:
                out[place + 1, k] = value
    await_bytes(r_last, top_rsem.at[7])
    for q in range(2):
        last = r_last[0, q].astype(F32)
        for zz in range(1, 8):
            last = last + r_last[zz, q].astype(F32)
        for i in range(2):
            out[0, 2 * q + i] = own_rows(last[8 * i : 8 * i + 8])


def on_device(
    right_side, top_right_side, leaf_upper, leaf_upper_mask, leaf_lower, leaf_lower_mask, cross_upper, cross_upper_mask,
    cross_lower, cross_lower_mask, top_upper, top_lower, leaf_upper_inverse, leaf_lower_inverse, top_upper_inverse,
    top_lower_inverse, leaf_sizes, top_sizes,
):
    in_hbm = pl.BlockSpec(memory_space=pl.ANY)
    in_smem = pl.BlockSpec(memory_space=pltpu.SMEM)
    in_vmem = pl.BlockSpec(memory_space=pltpu.VMEM)
    dma = pltpu.SemaphoreType.DMA
    out = pl.pallas_call(
        kernel,
        out_shape=jax.ShapeDtypeStruct((7, 4, 4, 128), F32),
        in_specs=[in_hbm] * 12 + [in_smem] * 6,
        out_specs=in_vmem,
        scratch_shapes=[
            pltpu.VMEM((42, 2, 4, 128, 128), BF),
            pltpu.VMEM((14, 4, 128, 128), F32),
            pltpu.VMEM((14, 4, 128, 256), BF),
            pltpu.VMEM((5, 4, 32, 128), F32),
            pltpu.VMEM((2, 4, 32, 128), F32),
            pltpu.VMEM((7, 32, 512), F32),
            pltpu.VMEM((5, 32, 256), F32),
            pltpu.VMEM((32, 256), F32),
            pltpu.VMEM((5, 4, 128, 128), BF),
            pltpu.VMEM((5, 4, 128, 128), BF),
            pltpu.VMEM((5, 4, 2, 128, 128), BF),
            pltpu.VMEM((4, 4, 32, 128), BF),
            pltpu.VMEM((4, 8, 4, 32, 128), BF),
            pltpu.VMEM((4, 2, 32, 128), BF),
            pltpu.VMEM((4, 4, 2, 32, 128), BF),
            pltpu.VMEM((4, 2, 2, 32, 128), BF),
            pltpu.VMEM((4, 8, 2, 32, 128), BF),
            pltpu.VMEM((5, 2, 32, 128), BF),
            pltpu.VMEM((2, 4, 2, 16, 128), F32),
            pltpu.VMEM((2, 4, 2, 16, 128), F32),
            pltpu.VMEM((2, 16, 128), BF),
            pltpu.VMEM((8, 16, 128), BF),
            pltpu.VMEM((2, 16, 128), BF),
            pltpu.VMEM((8, 2, 16, 128), BF),
            pltpu.VMEM((16, 16, 128), F32),
            pltpu.VMEM((4, 16, 128), F32),
            pltpu.VMEM((4, 2, 16, 128), BF),
            pltpu.VMEM((8, 2, 16, 128), BF),
            pltpu.VMEM((6, 4, 2, 8, 128), F32),
            pltpu.VMEM((6, 2, 2, 8, 128), F32),
        ]
        + [dma((n,)) for n in (20, 8, 8, 4, 4, 4, 4, 4, 4, 5, 5, 5, 5, 5, 5, 5, 5, 8, 8, 6, 1)],
        compiler_params=pltpu.CompilerParams(
            collective_id=0, has_side_effects=True, vmem_limit_bytes=58 * 1024 * 1024
        ),
    )(
        right_side, top_right_side, leaf_upper, leaf_lower, cross_upper, cross_lower, top_upper, top_lower,
        leaf_upper_inverse, leaf_lower_inverse, top_upper_inverse, top_lower_inverse,
        leaf_upper_mask[0, :, 0].T, leaf_lower_mask[0, :, 0].T,
        cross_upper_mask[0, :, 0].transpose(1, 2, 0), cross_lower_mask[0, :, 0].transpose(0, 2, 1),
        leaf_sizes[0].T, top_sizes,
    )
    return out[None, :5], out[5:]


def solution(mesh):
    in_specs = (
        P("rep", None, "row", None, None),
        P(None, "row", None, None),
        P("rep", None, "col", "row", None, None),
        P("rep", None, "col", "row"),
        P("rep", None, "col", "row", None, None),
        P("rep", None, "col", "row"),
        P("rep", None, "col", None, "row", None, None),
        P("rep", None, "col", None, "row"),
        P("rep", None, "col", None, "row", None, None),
        P("rep", None, "col", None, "row"),
        P(None, "col", "row", None, None),
        P(None, "col", "row", None, None),
        P("rep", None, "row", None, None),
        P("rep", None, "row", None, None),
        P(None, "row", None, None),
        P(None, "row", None, None),
        P("rep", None, "row"),
        P(None, "row"),
    )
    out_specs = (P("rep", None, "row", "col", None), P(None, "row", "col", None))
    return jax.shard_map(
        on_device, mesh=mesh, in_specs=in_specs, out_specs=out_specs, check_vma=False
    )
```

profile of v0, /device:TPU:1, one launch (start us, length us, event | category | flops | bytes accessed | tf_op | source)
XLA Modules:
  0.0 100.5 jit_solution(11286631895740476298)
XLA Ops:
  0.6 97.1 %shard_map.185 = f32[7,4,4,128]{3,2,1,0:T(4,128)} custom-call(f32[1,5,4,64,128]{4,3,2,1,0:T(8,128)} %rs.1, f32[2,4,64,128]{3,2,1,0:T(8,128)} %trs.1, bf16[1,10,1,4,128,128]{5,4,3,2,1,0:T(8,128)(2,1)} %lu.1, bf16[1,10,1,4,128,128]{5,4,3,2,1,0:T(8,128)(2,1)} %ll.1, bf16[1,5,1,2,4,128,128]{6,5,4,3,2,1,0:T(8,128)(2,1)} %cu.1, ...), custom_call_target="tpu_custom_call" | custom-call | tf_op jit(solution)/shard_map/pallas_call | solution.py:691
  97.7 1.3 %slice.7 = f32[2,4,4,128]{3,2,1,0:T(4,128)} slice(f32[7,4,4,128]{3,2,1,0:T(4,128)} %shard_map.185), slice={[5:7], [0:4], [0:4], [0:128]} | slice | bytes 32768 | tf_op jit(solution)/shard_map/slice | solution.py:739
  99.1 1.4 %slice_bitcast_fusion = f32[1,5,4,4,128]{4,3,2,1,0:T(4,128)} fusion(f32[7,4,4,128]{3,2,1,0:T(4,128)} %shard_map.185), kind=kLoop, calls=%fused_computation | loop fusion | bytes 81920 | tf_op jit(solution)/shard_map/broadcast_in_dim | solution.py:739
where the time goes:
time: 101 us; the launch traced here: 100 us
  Pallas kernels  97.1 us (96%)
  local copies, waits for them, and re-layouts  2.72 us (3%)
    pallas_call x1, Pallas kernels, on_device(): pl.pallas_call(kernel, out_shape=jax.ShapeDtypeStruct((7, 4, 4, 128), F32...  97.1 us

commit v1 on v0

--- a/solution.py
+++ b/solution.py
@@ -407,9 +407,9 @@
     shared["cu"].wait_recv()
     for a in range(2):
         subtract(5 + a, y0b, CU + a)
+    turn_share(0)
     turn_fold(1)
     turn_send(1)
-    turn_share(0)
     gather_receive(0)
     turn_ready(0)
     y1 = z_receive(0, parts)

time: 101 us -> 101 us (level)
  no operation moved by 1% of the time
where the time goes in v1:
time: 101 us
  Pallas kernels  97.3 us (96%)
  local copies, waits for them, and re-layouts  2.72 us (3%)
    pallas_call x1, Pallas kernels, on_device(): pl.pallas_call(kernel, out_shape=jax.ShapeDtypeStruct((7, 4, 4, 128), F32...  97.3 us

profile of v1, /device:TPU:1, one launch (start us, length us, event | category | flops | bytes accessed | tf_op | source)
XLA Modules:
  0.0 100.6 jit_solution(11321222861958408586)
XLA Ops:
  0.6 97.3 %shard_map.185 = f32[7,4,4,128]{3,2,1,0:T(4,128)} custom-call(f32[1,5,4,64,128]{4,3,2,1,0:T(8,128)} %rs.1, f32[2,4,64,128]{3,2,1,0:T(8,128)} %trs.1, bf16[1,10,1,4,128,128]{5,4,3,2,1,0:T(8,128)(2,1)} %lu.1, bf16[1,10,1,4,128,128]{5,4,3,2,1,0:T(8,128)(2,1)} %ll.1, bf16[1,5,1,2,4,128,128]{6,5,4,3,2,1,0:T(8,128)(2,1)} %cu.1, ...), custom_call_target="tpu_custom_call" | custom-call | tf_op jit(solution)/shard_map/pallas_call | solution.py:691
  97.9 1.3 %slice.7 = f32[2,4,4,128]{3,2,1,0:T(4,128)} slice(f32[7,4,4,128]{3,2,1,0:T(4,128)} %shard_map.185), slice={[5:7], [0:4], [0:4], [0:128]} | slice | bytes 32768 | tf_op jit(solution)/shard_map/slice | solution.py:739
  99.3 1.4 %slice_bitcast_fusion = f32[1,5,4,4,128]{4,3,2,1,0:T(4,128)} fusion(f32[7,4,4,128]{3,2,1,0:T(4,128)} %shard_map.185), kind=kLoop, calls=%fused_computation | loop fusion | bytes 81920 | tf_op jit(solution)/shard_map/broadcast_in_dim | solution.py:739
